TPU v7x, 32 devices: a whole 2x2x4 slice. The times are simulated.
32 devices in a mesh: dp: 2 (over x), ctx: 4 (over z), exp: 4 (over y, core).
Axes of the slice: x: 2, y: 2, z: 4, core: 2. Of those that a mesh axis runs over, the one named last changes fastest.
Arguments:
- tokens: bfloat16 [8, 2048, 1536], P(('dp', 'exp'), 'ctx'), may hold values from -6 to 6
- attn_gain: float32 [1536], replicated, may hold values from 0.5 to 1.5
- w_query: bfloat16 [1536, 1536], replicated, may hold values from -0.15625 to 0.15625
- key_matrix: bfloat16 [1536, 256], replicated, may hold values from -0.15625 to 0.15625
- value_matrix: bfloat16 [1536, 256], replicated, may hold values from -0.15625 to 0.15625
- w_out: bfloat16 [1536, 1536], replicated, may hold values from -2 to 2
- ffn_gain: float32 [1536], replicated, may hold values from 0.5 to 1.5
- expert_gate_up: bfloat16 [8, 1536, 1536], P('exp'), may hold values from -0.15625 to 0.15625
- expert_down: bfloat16 [8, 768, 1536], P('exp'), may hold values from -0.21875 to 0.21875
- expert_ids: int32 [8, 2048, 4], P(('dp', 'exp'), 'ctx'), may hold values from 0 to 7, all different within a row; in each aligned block of 512 rows (0 to 511, 512 to 1023, ..., all dimensions but the last counted through in order) at most 320 rows name the same one
- gate_weights: float32 [8, 2048, 4], P(('dp', 'exp'), 'ctx'), may hold values from 0.2 to 0.6
- span_order: int32 [8, 8], P(('dp', 'exp')), may hold values from 0 to 7, each once within a row
- out_grad: bfloat16 [8, 2048, 1536], P(('dp', 'exp'), 'ctx'), may hold values from -6 to 6
Outputs:
- layer_output: bfloat16 [8, 2048, 1536], P(('dp', 'exp'), 'ctx')
- tokens_grad: bfloat16 [8, 2048, 1536], P(('dp', 'exp'), 'ctx')
- attn_gain_grad: float32 [1536], P(('dp', 'ctx', 'exp'))
- w_query_grad: float32 [1536, 1536], P(('dp', 'ctx', 'exp'))
- w_key_grad: float32 [1536, 256], P(('dp', 'ctx', 'exp'))
- w_value_grad: float32 [1536, 256], P(('dp', 'ctx', 'exp'))
- w_out_grad: float32 [1536, 1536], P(('dp', 'ctx', 'exp'))
- ffn_gain_grad: float32 [1536], P(('dp', 'ctx', 'exp'))
- expert_gate_up_grad: float32 [8, 1536, 1536], P('exp', ('dp', 'ctx'))
- expert_down_grad: float32 [8, 768, 1536], P('exp', ('dp', 'ctx'))
Inputs may be any that keep to these rules, and one draw needn't show every extreme that they name: `expert_ids`: within the 512 rows of one device, each row names 4 different experts and no expert is named by more than 320 of them; in every draw some expert is named by exactly 320 rows of some such block. `span_order`: each row is a permutation of the 2 * 4 spans of 256 positions of its sequence.
All inputs are finite; a program needn't handle non-finite values.
Results may differ from a plain program's by a relative error of at most 0.028.
Values may be sent and summed in bfloat16 or wider, within the bound.
A program may use at most 320 MiB of HBM per device.

v0:
```python
import functools
import math

import jax
import jax.numpy as jnp
from jax import lax
from jax.experimental import pallas as pl
from jax.experimental.pallas import tpu as pltpu
from jax.sharding import PartitionSpec as P

MODEL_WIDTH = 1536
QUERY_HEADS = 12
KEY_VALUE_HEADS = 2
GROUP = QUERY_HEADS // KEY_VALUE_HEADS
HEAD_SIZE = 128
KV_WIDTH = KEY_VALUE_HEADS * HEAD_SIZE
FF = 768
TOPK = 4
EXP_DEV = 2
TOK_DEV = 512
HALF = 256

epsilon = 1e-06
rope_base = 1000000.0
masked_score = -1e30
score_scale = HEAD_SIZE ** (-0.5)
score_to_log2 = score_scale * math.log2(math.e)
gelu_c = math.sqrt(2.0 / math.pi)

f32 = jnp.float32
bf16 = jnp.bfloat16
NT = (((1,), (1,)), ((), ()))
TN = (((0,), (0,)), ((), ()))
VMEM_BYTES = 63 * 1024 * 1024
MESH = pl.DeviceIdType.MESH


def dot(a, b):
    return jnp.dot(a, b, preferred_element_type=f32)


def dot_nt(a, b):
    return lax.dot_general(a, b, NT, preferred_element_type=f32)


def dot_tn(a, b):
    return lax.dot_general(a, b, TN, preferred_element_type=f32)


def params(**more):
    return pltpu.CompilerParams(vmem_limit_bytes=VMEM_BYTES, **more)


def cost(flops, size, exps=0):
    return pl.CostEstimate(flops=int(flops) // 32, bytes_accessed=int(size) // 32, transcendentals=int(exps) // 32)


def whole(shape):
    return pl.BlockSpec(shape, lambda *_: (0,) * len(shape))


def rotate(values, cosine, signed_sine):
    return values * cosine + pltpu.roll(values, HEAD_SIZE // 2, 1) * signed_sine


def rotate_back(values, cosine, signed_sine):
    return values * cosine - pltpu.roll(values, HEAD_SIZE // 2, 1) * signed_sine


HEAD_ROWS = 16


class Gather:
    def __init__(self, own, slots, send_sem, recv_sem):
        self.own, self.slots, self.send_sem, self.recv_sem = own, slots, send_sem, recv_sem
        self.chips = lax.axis_size("exp") // 2
        exp = lax.axis_index("exp")
        core, chip = lax.rem(exp, 2), exp // 2
        self.other = {"exp": chip * 2 + 1 - core}
        self.ahead = [
            {"exp": lax.rem(chip + s, self.chips) * 2 + core} for s in range(self.chips)
        ]
        self.behind = [
            {"exp": lax.rem(chip + self.chips - s, self.chips) * 2 + core}
            for s in range(self.chips)
        ]

    def neighbours(self):
        if self.chips == 2:
            return [self.other, self.ahead[1]]
        return [self.other] + self.ahead[1:]

    def copy(self, slot):
        source, device = self.own, self.other
        if slot > 1 and slot % 2 == 0:
            source = self.slots.at[slot + 1]
        elif slot > 1:
            device = self.ahead[slot // 2]
        return remote(
            source, self.slots.at[slot], self.send_sem.at[slot], self.recv_sem.at[slot], device
        )

    def keep(self):
        return pltpu.make_async_copy(self.own, self.slots.at[0], self.recv_sem.at[0])

    def start(self):
        self.copy(1).start()
        for s in range(1, self.chips):
            self.copy(2 * s + 1).start()

    def cross(self):
        for s in range(1, self.chips):
            self.copy(2 * s + 1).wait_recv()
            self.copy(2 * s).start()

    def finish(self):
        self.copy(1).wait_recv()
        for s in range(1, self.chips):
            self.copy(2 * s).wait_recv()
        self.finish_sends()

    def finish_sends(self):
        for slot in range(1, 2 * self.chips):
            self.copy(slot).wait_send()


def routes(ids_ref, gates_ref, place_cols, routing):
    rows = ids_ref.shape[1]
    lane = lax.broadcasted_iota(jnp.int32, (rows, HEAD_SIZE), 1).astype(f32)
    both = jnp.concatenate([ids_ref[...].astype(f32), gates_ref[...]], axis=0).T
    member = jnp.zeros((rows, HEAD_SIZE), f32)
    gates = jnp.zeros((rows, HEAD_SIZE), f32)
    for k in range(TOPK):
        hit = both[:, k : k + 1] == lane
        member = jnp.where(hit, 1.0, member)
        gates = jnp.where(hit, both[:, TOPK + k : TOPK + k + 1], gates)
    later = lax.broadcasted_iota(jnp.int32, (rows, rows), 0)
    earlier = later > lax.broadcasted_iota(jnp.int32, (rows, rows), 1)
    place = dot(earlier.astype(bf16), member.astype(bf16))
    place = jnp.where(member > 0.0, place, -1.0)
    place_cols[...] = place
    routing[0] = place.T[: routing.shape[1], :]
    routing[1] = gates.T[: routing.shape[1], :]


def forward_kernel(
    n, x_ref, gain_ref, wk_ref, wv_ref, cos_ref, sin_ref, qpos_ref, kpos_ref, ffn_gain_ref, wq_hbm,
    wo_hbm, g_hbm, ids_ref, gates_ref, normed_ref, q_ref, kv_ref, att_ref, att_low_ref, lse_ref,
    mid_ref, nf_ref, g_all, place_cols_all, routing_all, wq_ref, wo_ref, tops, totals, place_cols,
    routing, load_sem, send_sem, recv_sem, *gather_sems,
):
    load_q = pltpu.make_async_copy(wq_hbm, wq_ref, load_sem.at[0])
    load_o = pltpu.make_async_copy(wo_hbm, wo_ref, load_sem.at[1])
    load_q.start()
    load_o.start()
    ctx = Axis("ctx")
    gathers = [
        Gather(g_hbm, g_all, *gather_sems[0:2]),
        Gather(place_cols, place_cols_all, *gather_sems[2:4]),
        Gather(routing, routing_all, *gather_sems[4:6]),
    ]
    signal_and_wait(ctx.neighbours() + gathers[0].neighbours())

    def pass_on(step):
        return remote(
            kv_ref.at[step], kv_ref.at[step + 1], send_sem.at[step], recv_sem.at[step], ctx.next
        )

    rows = x_ref.shape[0]
    x = x_ref[...].astype(f32)
    r = lax.rsqrt(jnp.mean(x * x, axis=-1, keepdims=True) + epsilon)
    normed_ref[...] = (x * r * gain_ref[...]).astype(bf16)
    normed = normed_ref[...]
    cosine, sine = cos_ref[...], sin_ref[...]
    keys = dot(normed, wk_ref[...])
    for head in range(KEY_VALUE_HEADS):
        span = slice(head * HEAD_SIZE, (head + 1) * HEAD_SIZE)
        kv_ref[0, :, span] = rotate(keys[:, span], cosine, sine).astype(bf16)
    kv_ref[0, :, KV_WIDTH:] = dot(normed, wv_ref[...]).astype(bf16)
    pass_on(0).start()
    routes(ids_ref, gates_ref, place_cols, routing)
    for gather in gathers:
        gather.start()
        gather.keep().start()
    load_q.wait()
    for start in range(0, MODEL_WIDTH, WIDTH_TILE):
        queries = dot(normed, wq_ref[:, start : start + WIDTH_TILE])
        for offset in range(0, WIDTH_TILE, HEAD_SIZE):
            span = slice(start + offset, start + offset + HEAD_SIZE)
            part = queries[:, offset : offset + HEAD_SIZE]
            q_ref[:, span] = rotate(part, cosine, sine).astype(bf16)

    for step in range(n):
        if step:
            pass_on(step - 1).wait_recv()
            if step < n - 1:
                pass_on(step).start()
        allowed = kpos_ref[step] <= qpos_ref[...]

        def one_group(group, carry):
            keys = kv_ref[step, :, pl.ds(pl.multiple_of(group * HEAD_SIZE, HEAD_SIZE), HEAD_SIZE)]
            start = pl.multiple_of(KV_WIDTH + group * HEAD_SIZE, HEAD_SIZE)
            values = kv_ref[step, :, pl.ds(start, HEAD_SIZE)]
            for member in range(GROUP):
                head = group * GROUP + member
                columns = pl.ds(pl.multiple_of(head * HEAD_SIZE, HEAD_SIZE), HEAD_SIZE)
                lane = slice(member, member + 1)
                scores = jnp.where(allowed, dot_nt(q_ref[:, columns], keys), masked_score)
                top = jnp.max(scores, axis=-1, keepdims=True) * score_to_log2
                if step:
                    before = tops[group, :, lane]
                    top = jnp.maximum(before, top)
                    rescale = jnp.exp2(before - top)
                weights = jnp.exp2(scores * score_to_log2 - top)
                total = jnp.sum(weights, axis=-1, keepdims=True)
                out = dot(weights.astype(bf16), values)
                if step:
                    total += totals[group, :, lane] * rescale
                    out += att_ref[:, columns] * rescale
                if step < n - 1:
                    tops[group, :, lane] = top
                    totals[group, :, lane] = total
                else:
                    out /= total
                    att_low_ref[:, columns] = out.astype(bf16)
                    tops[group, :, lane] = top + jnp.log2(total)
                att_ref[:, columns] = out
            return carry

        lax.fori_loop(0, KEY_VALUE_HEADS, one_group, 0)
    for group in range(KEY_VALUE_HEADS):
        lse_ref[group * GROUP : (group + 1) * GROUP, :] = tops[group].T[:GROUP, :]
    lse_ref[QUERY_HEADS:, :] = jnp.zeros((HEAD_ROWS - QUERY_HEADS, rows), f32)
    for gather in gathers:
        gather.cross()
    load_o.wait()
    half = rows // 2
    for part in range(2):
        band = slice(part * half, (part + 1) * half)
        mid = x_ref[band, :].astype(f32) + dot(att_low_ref[band, :], wo_ref[...])
        mid_ref[band, :] = mid
        r = lax.rsqrt(jnp.mean(mid * mid, axis=-1, keepdims=True) + epsilon)
        nf_ref[band, :] = (mid * r * ffn_gain_ref[...]).astype(bf16)
    for step in range(n - 1):
        pass_on(step).wait_send()
    for gather in gathers:
        gather.keep().wait()
        gather.finish()


def forward_to_experts(
    x, gain, wk, wv, cosine, sine, qpos_col, kpos_rows, ffn_gain, wq, wo, g, ids, gates
):
    exp_size = lax.axis_size("exp")
    routing = (2, EXP_DEV * exp_size, x.shape[0])
    rows, n = x.shape[0], kpos_rows.shape[0]
    vmem = pl.BlockSpec(memory_space=pltpu.VMEM)
    hbm = pl.BlockSpec(memory_space=pl.ANY)
    wide = (rows, MODEL_WIDTH)
    return pl.pallas_call(
        functools.partial(forward_kernel, n),
        in_specs=[vmem] * 9 + [hbm] * 3 + [vmem] * 2,
        out_specs=(vmem,) * 8 + (hbm,) * 3,
        out_shape=(
            jax.ShapeDtypeStruct(wide, bf16),
            jax.ShapeDtypeStruct(wide, bf16),
            jax.ShapeDtypeStruct((n, rows, 2 * KV_WIDTH), bf16),
            jax.ShapeDtypeStruct(wide, f32),
            jax.ShapeDtypeStruct(wide, bf16),
            jax.ShapeDtypeStruct((HEAD_ROWS, rows), f32),
            jax.ShapeDtypeStruct(wide, f32),
            jax.ShapeDtypeStruct(wide, bf16),
            jax.ShapeDtypeStruct((exp_size, *g.shape), bf16),
            jax.ShapeDtypeStruct((exp_size, rows, HEAD_SIZE), f32),
            jax.ShapeDtypeStruct((exp_size, *routing), f32),
        ),
        scratch_shapes=[
            pltpu.VMEM((MODEL_WIDTH, MODEL_WIDTH), bf16),
            pltpu.VMEM((MODEL_WIDTH, MODEL_WIDTH), bf16),
            pltpu.VMEM((KEY_VALUE_HEADS, rows, HEAD_SIZE), f32),
            pltpu.VMEM((KEY_VALUE_HEADS, rows, HEAD_SIZE), f32),
            pltpu.VMEM((rows, HEAD_SIZE), f32),
            pltpu.VMEM(routing, f32),
            pltpu.SemaphoreType.DMA((2,)),
            pltpu.SemaphoreType.DMA((n - 1,)),
            pltpu.SemaphoreType.DMA((n - 1,)),
        ]
        + [pltpu.SemaphoreType.DMA((exp_size,))] * 6,
        compiler_params=params(collective_id=3, has_side_effects=True),
        cost_estimate=cost(
            4 * n * rows * rows * MODEL_WIDTH + 5 * rows * MODEL_WIDTH * MODEL_WIDTH, 4e7,
            n * rows * rows * QUERY_HEADS,
        ),
        name="forward_to_experts",
    )(x, gain, wk, wv, cosine, sine, qpos_col, kpos_rows, ffn_gain, wq, wo, g, ids, gates)


FF_TILE = 256
WIDTH_TILE = 512


def expert_kernel(
    place_cols_ref, routing_ref, nf_hbm, g_ref, wgu_ref, wd_ref, dx_chip, y_chip, dx_far,
    y_far, rows_ref, hidden_ref, slot_grad_ref, pg_ref, x_all, x_ref, place, result, rows_grad,
    dx_out, y_out, dx_came, y_came, load_sem, gather_send, gather_recv, back_send, back_recv,
):
    block, expert = pl.program_id(0), pl.program_id(1)
    capacity = rows_ref.shape[-2]
    tokens = x_ref.shape[0]
    gather = Gather(nf_hbm, x_all, gather_send, gather_recv)
    chips = gather.chips

    def load(source):
        copy = pltpu.make_async_copy(source, x_ref, load_sem.at[0])
        copy.start()
        copy.wait()

    def back(slot):
        return [
            remote(out, came.at[slot], back_send.at[i, slot], back_recv.at[i, slot], gather.other)
            for i, (out, came) in enumerate(((dx_out, dx_came), (y_out, y_came)))
        ]

    @pl.when((block == 0) & (expert == 0))
    def _():
        signal_and_wait(gather.neighbours())
        gather.start()
        load(nf_hbm)

    @pl.when((block == 1) & (expert == 0))
    def _():
        gather.copy(1).wait_recv()
        load(x_all.at[1])

    for s in range(1, chips):

        @pl.when((block == 2 * s) & (expert == 0))
        def _():
            if s == 1:
                gather.cross()
            gather.copy(2 * s).wait_recv()
            load(x_all.at[2 * s])

        @pl.when((block == 2 * s + 1) & (expert == 0))
        def _():
            load(x_all.at[2 * s + 1])

    mine = lax.axis_index("exp") * EXP_DEV + expert
    slot_r = lax.broadcasted_iota(jnp.int32, (capacity, tokens), 0).astype(f32)
    slot_c = lax.broadcasted_iota(jnp.int32, (tokens, capacity), 1).astype(f32)
    match = slot_r == routing_ref[0, 0, pl.ds(mine, 1), :]
    pick = match.astype(bf16)
    lane = lax.broadcasted_iota(jnp.int32, (tokens, HEAD_SIZE), 1)
    place_col = jnp.sum(jnp.where(lane == mine, place_cols_ref[0], 0.0), axis=1, keepdims=True)
    place[expert] = (slot_c == place_col).astype(bf16)
    gate_row = routing_ref[0, 1, pl.ds(mine, 1), :]
    gates = jnp.sum(jnp.where(match, gate_row, 0.0), axis=1, keepdims=True)
    for start in range(0, MODEL_WIDTH, WIDTH_TILE):
        span = slice(start, start + WIDTH_TILE)
        rows_ref[0, 0, :, span] = dot(pick, x_ref[:, span]).astype(bf16)
        slot_grad_ref[0, 0, :, span] = (dot(pick, g_ref[0, :, span]) * gates).astype(bf16)
    rows = rows_ref[0, 0]
    slot_grad = slot_grad_ref[0, 0]
    for start in range(0, FF, FF_TILE):
        span = slice(start, start + FF_TILE)
        up_span = slice(FF + start, FF + start + FF_TILE)
        gate = dot(rows, wgu_ref[0, :, span])
        up = dot(rows, wgu_ref[0, :, up_span])
        hidden_grad = dot_nt(slot_grad, wd_ref[0, span, :])
        square = gate * gate
        tangent = jnp.tanh(gate * (gelu_c + (gelu_c * 0.044715) * square))
        half_plus = 0.5 + 0.5 * tangent
        activated = gate * half_plus
        slope = half_plus + activated * (1.0 - tangent) * (
            gelu_c + (3.0 * 0.044715 * gelu_c) * square
        )
        hidden_ref[0, 0, :, span] = (activated * up).astype(bf16)
        pg_ref[0, 0, :, span] = (hidden_grad * up * slope).astype(bf16)
        pg_ref[0, 0, :, up_span] = (hidden_grad * activated).astype(bf16)
    hidden = hidden_ref[0, 0]
    projected_grad = pg_ref[0, 0]
    for start in range(0, MODEL_WIDTH, WIDTH_TILE):
        span = slice(start, start + WIDTH_TILE)
        result[expert, :, span] = (dot(hidden, wd_ref[0, :, span]) * gates).astype(bf16)
        rows_grad[expert, :, span] = dot_nt(projected_grad, wgu_ref[0, span, :]).astype(bf16)

    last = expert == EXP_DEV - 1
    for sent in [1] + [2 * s for s in range(1, chips)]:

        @pl.when(last & (block == sent + 1))
        def _():
            for copy in back(sent // 2):
                copy.wait_send()

    @pl.when(last)
    def _():
        both = jnp.concatenate([place[e] for e in range(EXP_DEV)], axis=1)
        for start in range(0, MODEL_WIDTH, WIDTH_TILE):
            span = slice(start, start + WIDTH_TILE)
            for out_ref, terms in ((y_out, result), (dx_out, rows_grad)):
                stacked = terms[:, :, span].reshape(EXP_DEV * capacity, WIDTH_TILE)
                out_ref[:, span] = dot(both, stacked).astype(bf16)

    @pl.when(last & (block == 0))
    def _():
        dx_chip[...] = dx_out[...]
        y_chip[...] = y_out[...]

    for sent in [1] + [2 * s for s in range(1, chips)]:

        @pl.when(last & (block == sent))
        def _():
            for copy in back(sent // 2):
                copy.start()

    def add(target, own, came):
        for start in range(0, tokens, HEAD_SIZE):
            band = slice(start, start + HEAD_SIZE)
            total = own[band, :].astype(f32) + came[band, :].astype(f32)
            target[band, :] = total.astype(bf16)

    for s in range(1, chips):

        @pl.when(last & (block == 2 * s + 1))
        def _():
            for copy in back(s):
                copy.wait_recv()
            add(dx_far.at[s - 1], dx_out, dx_came.at[s])
            add(y_far.at[s - 1], y_out, y_came.at[s])

    @pl.when(last & (block == 2 * chips - 1))
    def _():
        for copy in back(0):
            copy.wait_recv()
        add(dx_chip, dx_chip, dx_came.at[0])
        add(y_chip, y_chip, y_came.at[0])
        gather.finish_sends()


def expert_blocks(capacity, place_cols, routing, nf, g_all, wgu, wd):
    blocks, tokens, _ = g_all.shape
    chips = blocks // 2
    kept_shapes = tuple(
        jax.ShapeDtypeStruct((EXP_DEV, blocks, capacity, width), bf16)
        for width in (MODEL_WIDTH, FF, MODEL_WIDTH, 2 * FF)
    )
    kept_specs = tuple(
        pl.BlockSpec((1, 1, capacity, s.shape[-1]), lambda b, e: (e, b, 0, 0)) for s in kept_shapes
    )
    flops = blocks * EXP_DEV * 2 * capacity * (4 * tokens * MODEL_WIDTH + 9 * MODEL_WIDTH * FF)
    wide = (tokens, MODEL_WIDTH)
    result = jax.ShapeDtypeStruct(wide, bf16)
    far = jax.ShapeDtypeStruct((chips - 1, *wide), bf16)
    hbm = pl.BlockSpec(memory_space=pl.ANY)

    def once(shape):
        return pl.BlockSpec(
            shape, lambda b, e: (0,) * len(shape), pipeline_mode=pl.Buffered(1)
        )

    return pl.pallas_call(
        expert_kernel,
        grid=(blocks, EXP_DEV),
        in_specs=[
            pl.BlockSpec((1, tokens, HEAD_SIZE), lambda b, e: (b, 0, 0)),
            pl.BlockSpec((1, *routing.shape[1:]), lambda b, e: (b, 0, 0, 0)),
            hbm,
            pl.BlockSpec((1, tokens, MODEL_WIDTH), lambda b, e: (b, 0, 0)),
            pl.BlockSpec((1, MODEL_WIDTH, 2 * FF), lambda b, e: (e, 0, 0)),
            pl.BlockSpec((1, FF, MODEL_WIDTH), lambda b, e: (e, 0, 0)),
        ],
        out_specs=(once(wide), once(wide), once(far.shape), once(far.shape)) + kept_specs + (hbm,),
        out_shape=(result, result, far, far)
        + kept_shapes
        + (jax.ShapeDtypeStruct((blocks, *wide), bf16),),
        scratch_shapes=[
            pltpu.VMEM(wide, bf16),
            pltpu.VMEM((EXP_DEV, tokens, capacity), bf16),
            pltpu.VMEM((EXP_DEV, capacity, MODEL_WIDTH), bf16),
            pltpu.VMEM((EXP_DEV, capacity, MODEL_WIDTH), bf16),
            pltpu.VMEM(wide, bf16),
            pltpu.VMEM(wide, bf16),
            pltpu.VMEM((chips, *wide), bf16),
            pltpu.VMEM((chips, *wide), bf16),
            pltpu.SemaphoreType.DMA((1,)),
            pltpu.SemaphoreType.DMA((blocks,)),
            pltpu.SemaphoreType.DMA((blocks,)),
            pltpu.SemaphoreType.DMA((2, chips)),
            pltpu.SemaphoreType.DMA((2, chips)),
        ],
        compiler_params=params(collective_id=4, has_side_effects=True),
        cost_estimate=cost(flops, 6e7),
        name="expert_blocks",
    )(place_cols, routing, nf, g_all, wgu, wd)


GRAD_TILE = 384


def weight_grad_kernel(chunk_ref, a_ref, b_ref, out_ref):
    out_ref[0] = dot_tn(a_ref[0], b_ref[0]).astype(bf16)


def weight_grad(first, experts, chunk, size, a, b):
    slots, width = a.shape[1], b.shape[-1]
    tiles = size // GRAD_TILE
    return pl.pallas_call(
        weight_grad_kernel,
        grid_spec=pltpu.PrefetchScalarGridSpec(
            num_scalar_prefetch=1,
            grid=(experts, tiles),
            in_specs=[
                pl.BlockSpec((1, slots, GRAD_TILE), lambda e, t, c: (first + e, 0, c[0] * tiles + t)),
                pl.BlockSpec((1, slots, width), lambda e, t, c: (first + e, 0, 0)),
            ],
            out_specs=pl.BlockSpec((1, GRAD_TILE, width), lambda e, t, c: (e, t, 0)),
        ),
        out_shape=jax.ShapeDtypeStruct((experts, size, width), bf16),
        compiler_params=params(),
        cost_estimate=cost(2 * experts * slots * size * width, 2e7),
        name="weight_grad",
    )(chunk.reshape(1).astype(jnp.int32), a, b)


def other_weight_grads_kernel(
    dp_ref, rows_ref, pg_ref, hidden_ref, slot_grad_ref, theirs_ref, mine0_ref, mine1_ref,
    other_down_ref, mine_down_ref,
):
    step = pl.program_id(0)
    for first, out_ref in ((0, theirs_ref), (2, mine0_ref), (4, mine1_ref)):

        @pl.when((step == first) | (step == first + 1))
        def _():
            out_ref[...] = dot_tn(rows_ref[0], pg_ref[0]).astype(bf16)

    for place, out_ref in enumerate((other_down_ref, mine_down_ref)):

        @pl.when((step == 6 + place) | (step == 8 + place))
        def _():
            out_ref[0] = dot_tn(hidden_ref[0], slot_grad_ref[0]).astype(bf16)


def other_weight_grads(dp_here, dp_size, slot_rows, pg, hidden, slot_grad):
    assert dp_size == 2 and MODEL_WIDTH // dp_size == 2 * GRAD_TILE and FF // dp_size == GRAD_TILE
    slots = slot_rows.shape[1]
    half = (2 * GRAD_TILE, 2 * FF)

    def gate_up_rows(t, d):
        t = jnp.minimum(t, 5)
        expert = jnp.where((t == 2) | (t == 3), 0, 1)
        place = jnp.where(t < 2, 1 - d[0], d[0])
        return expert, 0, place * 2 + t % 2

    def gate_up_right(t, d):
        return gate_up_rows(t, d)[0], 0, 0

    def down_rows(t, d):
        t = jnp.maximum(t, 6) - 6
        return t // 2, 0, jnp.where(t % 2 == 0, 1 - d[0], d[0])

    def down_right(t, d):
        return down_rows(t, d)[0], 0, 0

    def piece(first):
        return pl.BlockSpec((GRAD_TILE, 2 * FF), lambda t, d: (jnp.clip(t - first, 0, 1), 0))

    def down(first):
        return pl.BlockSpec(
            (1, GRAD_TILE, MODEL_WIDTH), lambda t, d: (jnp.clip((t - first) // 2, 0, 1), 0, 0)
        )

    return pl.pallas_call(
        other_weight_grads_kernel,
        grid_spec=pltpu.PrefetchScalarGridSpec(
            num_scalar_prefetch=1,
            grid=(10,),
            in_specs=[
                pl.BlockSpec((1, slots, GRAD_TILE), gate_up_rows),
                pl.BlockSpec((1, slots, 2 * FF), gate_up_right),
                pl.BlockSpec((1, slots, GRAD_TILE), down_rows),
                pl.BlockSpec((1, slots, MODEL_WIDTH), down_right),
            ],
            out_specs=(piece(0), piece(2), piece(4), down(6), down(7)),
        ),
        out_shape=(jax.ShapeDtypeStruct(half, bf16),) * 3
        + (jax.ShapeDtypeStruct((EXP_DEV, GRAD_TILE, MODEL_WIDTH), bf16),) * 2,
        compiler_params=params(),
        cost_estimate=cost(10 * 2 * slots * GRAD_TILE * 2 * FF, 5e7),
        name="other_weight_grads",
    )(dp_here.reshape(1).astype(jnp.int32), slot_rows, pg, hidden, slot_grad)


def middle_kernel(*refs):
    count = len(refs) - 13
    parts = refs[:count]
    mid_ref, g_ref, gain_ref, wo_ref, att_ref, att_low_ref = refs[count : count + 6]
    mg_ref, ag_ref, delta_ref, dgain_ref, wo_grad_ref, mgl_ref, delta_cols = refs[count + 6 :]
    rows = mid_ref.shape[0]
    half = rows // 2
    lane = lax.broadcasted_iota(jnp.int32, (half, HEAD_SIZE), 1)
    dgain = jnp.zeros((1, MODEL_WIDTH), f32)
    for part in range(2):
        band = slice(part * half, (part + 1) * half)
        nf_grad = parts[0][band, :].astype(f32)
        for other in parts[1:]:
            nf_grad += other[band, :].astype(f32)
        mid = mid_ref[band, :]
        r = lax.rsqrt(jnp.mean(mid * mid, axis=-1, keepdims=True) + epsilon)
        u = nf_grad * gain_ref[...]
        inner = jnp.mean(u * mid, axis=-1, keepdims=True)
        grad = g_ref[band, :].astype(f32) + r * u - mid * (r * r * r * inner)
        dgain += jnp.sum(nf_grad * mid * r, axis=0, keepdims=True)
        mg_ref[band, :] = grad
        low = grad.astype(bf16)
        mgl_ref[band, :] = low
        att_grad = dot_nt(low, wo_ref[...]).astype(bf16)
        ag_ref[band, :] = att_grad
        delta = jnp.zeros((half, HEAD_SIZE), f32)
        for head in range(QUERY_HEADS):
            span = slice(head * HEAD_SIZE, (head + 1) * HEAD_SIZE)
            one = jnp.sum(att_grad[:, span].astype(f32) * att_ref[band, span], axis=-1, keepdims=True)
            delta = jnp.where(lane == head, one, delta)
        delta_cols[band, :] = delta
    dgain_ref[...] = dgain
    delta_ref[...] = delta_cols[...].T[: delta_ref.shape[0], :]
    store_by_owner(wo_grad_ref, att_low_ref, mgl_ref[...])


def middle_backward(parts, mid, g, gain, wo, att, att_low):
    rows = mid.shape[0]
    return pl.pallas_call(
        middle_kernel,
        out_shape=(
            jax.ShapeDtypeStruct((rows, MODEL_WIDTH), f32),
            jax.ShapeDtypeStruct((rows, MODEL_WIDTH), bf16),
            jax.ShapeDtypeStruct((HEAD_ROWS, rows), f32),
            jax.ShapeDtypeStruct((1, MODEL_WIDTH), f32),
            jax.ShapeDtypeStruct((MODEL_WIDTH, MODEL_WIDTH), bf16),
        ),
        scratch_shapes=[
            pltpu.VMEM((rows, MODEL_WIDTH), bf16),
            pltpu.VMEM((rows, HEAD_SIZE), f32),
        ],
        compiler_params=params(),
        cost_estimate=cost(4 * rows * MODEL_WIDTH * MODEL_WIDTH, 3e7),
        name="middle_backward",
    )(*parts, mid, g, gain, wo, att, att_low)


def signal_and_wait(neighbours):
    barrier = pltpu.get_barrier_semaphore()
    for neighbour in neighbours:
        pl.semaphore_signal(barrier, inc=1, device_id=neighbour, device_id_type=MESH)
    pl.semaphore_wait(barrier, len(neighbours))


def remote(source, target, send_sem, recv_sem, device):
    return pltpu.make_async_remote_copy(
        src_ref=source, dst_ref=target, send_sem=send_sem, recv_sem=recv_sem,
        device_id=device, device_id_type=MESH,
    )


class Axis:
    def __init__(self, name):
        if name in ("dp", "ctx"):
            self.count, self.me = lax.axis_size(name), lax.axis_index(name)
            place = lambda i: {name: i}
        else:
            exp = lax.axis_index("exp")
            core, chip = lax.rem(exp, 2), exp // 2
            if name == "core":
                self.count, self.me = 2, core
                place = lambda i: {"exp": chip * 2 + i}
            else:
                self.count, self.me = lax.axis_size("exp") // 2, chip
                place = lambda i: {"exp": i * 2 + core}
        self.place = place
        self.next = place(lax.rem(self.me + 1, self.count))
        self.last = place(lax.rem(self.me + self.count - 1, self.count))

    def neighbours(self):
        return [self.next] if self.count == 2 else [self.next, self.last]

    def others(self):
        return [self.place(lax.rem(self.me + s, self.count)) for s in range(1, self.count)]


class Direct:
    def __init__(self, axis, source, rows, recv, send_sem, recv_sem):
        self.axis, self.count, self.source, self.rows = axis, 2, source, rows
        self.recv, self.send_sem, self.recv_sem = recv, send_sem, recv_sem

    def part(self, place):
        return pl.ds(pl.multiple_of(place * self.rows, self.rows), self.rows)

    def copies(self):
        axis, out = self.axis, []
        for s in range(1, axis.count):
            place = lax.rem(axis.me + s, axis.count)
            out.append(
                remote(
                    self.source.at[self.part(place), :], self.recv.at[s - 1],
                    self.send_sem.at[s - 1], self.recv_sem.at[s - 1], axis.place(place),
                )
            )
        return out

    def hop(self, hop):
        if hop == 0:
            for copy in self.copies():
                copy.start()
            return None
        total = self.source[self.part(self.axis.me), :].astype(f32)
        for i, copy in enumerate(self.copies()):
            copy.wait_recv()
            total += self.recv[i].astype(f32)
        return total

    def finish(self):
        for copy in self.copies():
            copy.wait_send()


class Ring:
    def __init__(self, axis, terms, rows, send, recv, send_sem, recv_sem, first=None, own=False):
        self.axis, self.count, self.terms, self.rows = axis, axis.count, terms, rows
        self.first, self.own = terms[0] if first is None else first, own
        self.send, self.recv, self.send_sem, self.recv_sem = send, recv, send_sem, recv_sem

    def here(self, hop):
        part = lax.rem(self.axis.me + self.count - 1 - hop, self.count)
        return pl.ds(pl.multiple_of(part * self.rows, self.rows), self.rows)

    def copy(self, hop):
        if len(self.terms) > 1:
            source = self.send.at[hop]
        elif hop == 0:
            source = self.first.at[self.here(0), :]
        else:
            source = self.send.at[hop - 1]
        return remote(
            source, self.recv.at[hop], self.send_sem.at[hop], self.recv_sem.at[hop], self.axis.next
        )

    def hop(self, hop):
        if hop == 0 and len(self.terms) == 1:
            self.copy(0).start()
            return None
        here = slice(0, self.rows) if self.own else self.here(hop)
        total = self.terms[0][here, :].astype(f32)
        for term in self.terms[1:]:
            total += term[here, :].astype(f32)
        if hop:
            self.copy(hop - 1).wait_recv()
            total += self.recv[hop - 1].astype(f32)
        if hop < self.count - 1:
            self.send[hop - (len(self.terms) == 1)] = total.astype(bf16)
            self.copy(hop).start()
        return total

    def finish(self):
        for hop in range(self.count - 1):
            self.copy(hop).wait_send()


def attention_back_kernel(
    n, q_ref, ag_ref, kv_ref, lse_ref, delta_ref, kpos_ref, qpos_ref, cos_ref, sin_ref, mine_hbm,
    came_hbm, wo_grad_hbm, next_ref, next_mine_ref, down_ref, down_mine_ref, dql_ref, dkv_ref,
    share_ref, next_sum_ref, down_sum_ref, wo_sum_ref, next_came, down_came, next_mine, down_mine,
    mine_ref, came_ref, wo_grad_ref, dq_acc, held, send, recv, send_sem, recv_sem, next_sem,
    load_sem, *scratch,
):
    ctx, core, chip = Axis("ctx"), Axis("core"), Axis("chip")
    right, across = ctx.next, Axis("dp").next
    signal_and_wait(ctx.neighbours() + core.neighbours() + chip.neighbours() + [across])
    core_rows = wo_grad_ref.shape[0]
    own_rows = pl.ds(pl.multiple_of(core.me * core_rows, core_rows), core_rows)
    wo_chain = Chain(
        [
            Ring(core, [wo_grad_ref], core_rows, *scratch[:4], wo_grad_hbm, True),
            Ring(chip, [scratch[4]], core_rows // chip.count, *scratch[5:9]),
        ],
        [scratch[4], wo_sum_ref],
    )
    ring = Ring(ctx, [mine_ref, came_ref], share_ref.shape[0], *scratch[9:])
    first_loads = [
        pltpu.make_async_copy(source, target, load_sem.at[i])
        for i, (source, target) in enumerate(
            ((mine_hbm, mine_ref), (came_hbm, came_ref), (wo_grad_hbm.at[own_rows, :], wo_grad_ref))
        )
    ]
    for load in first_loads:
        load.start()
    exchanges, loads = [], []
    for i, (source, target, mine_hbm, mine) in enumerate(
        (
            (next_ref, next_came, next_mine_ref, next_mine),
            (down_ref.at[0], down_came, down_mine_ref.at[0], down_mine),
        )
    ):
        exchanges.append(remote(source, target, next_sem.at[i, 0], next_sem.at[i, 1], across))
        loads.append(pltpu.make_async_copy(mine_hbm, mine, next_sem.at[i, 2]))
        exchanges[i].start()
        loads[i].start()
    wo_chain.step()
    for load in first_loads:
        load.wait()
    ring.hop(0)

    def dkv_copy(step, group):
        return remote(
            send.at[group, step], recv.at[group, step], send_sem.at[group, step],
            recv_sem.at[group, step], right,
        )

    qpos = qpos_ref[...].astype(f32)
    for step in range(n):
        back = (step + 1) % n
        kpos = jnp.broadcast_to(kpos_ref[back].astype(f32), (8, kpos_ref.shape[-1])).T[:, :1]

        def one_group(group, carry):
            keys = kv_ref[back, :, pl.ds(pl.multiple_of(group * HEAD_SIZE, HEAD_SIZE), HEAD_SIZE)]
            start = pl.multiple_of(KV_WIDTH + group * HEAD_SIZE, HEAD_SIZE)
            values = kv_ref[back, :, pl.ds(start, HEAD_SIZE)]
            dk = dv = None
            for member in range(GROUP):
                head = group * GROUP + member
                columns = pl.ds(pl.multiple_of(head * HEAD_SIZE, HEAD_SIZE), HEAD_SIZE)
                q, ag = q_ref[:, columns], ag_ref[:, columns]
                scores = dot_nt(keys, q)
                weights = jnp.exp2(scores * score_to_log2 - lse_ref[pl.ds(head, 1), :])
                weights = jnp.where(kpos <= qpos, weights, 0.0)
                weights_grad = dot_nt(values, ag)
                score_grad = weights * (weights_grad - delta_ref[pl.ds(head, 1), :]) * score_scale
                score_grad = score_grad.astype(bf16)
                dv_part = dot(weights.astype(bf16), ag)
                dk_part = dot(score_grad, q)
                dv = dv_part if dv is None else dv + dv_part
                dk = dk_part if dk is None else dk + dk_part
                dq = dot_tn(score_grad, keys)
                if step:
                    dq += dq_acc[:, columns]
                dq_acc[:, columns] = dq
            held[group] = jnp.concatenate([dk, dv], axis=1)
            return carry

        lax.fori_loop(0, KEY_VALUE_HEADS, one_group, 0)
        for group in range(KEY_VALUE_HEADS):
            dkv = held[group]
            if step:
                dkv_copy(step - 1, group).wait_recv()
                dkv += recv[group, step - 1].astype(f32)
            if step < n - 1:
                send[group, step] = dkv.astype(bf16)
                dkv_copy(step, group).start()
            else:
                for place in range(2):
                    start = place * KV_WIDTH + group * HEAD_SIZE
                    part = dkv[:, place * HEAD_SIZE : (place + 1) * HEAD_SIZE]
                    dkv_ref[:, start : start + HEAD_SIZE] = part.astype(bf16)
        if step < n - 2:
            ring.hop(step + 1)
        wo_chain.step(2 if step == 0 else 1)
    cosine, sine = cos_ref[...], sin_ref[...]
    for head in range(QUERY_HEADS):
        span = slice(head * HEAD_SIZE, (head + 1) * HEAD_SIZE)
        dql_ref[:, span] = rotate_back(dq_acc[:, span], cosine, sine).astype(bf16)
    share_ref[...] = ring.hop(n - 1)
    ring.finish()
    for step in range(n - 1):
        for group in range(KEY_VALUE_HEADS):
            dkv_copy(step, group).wait_send()
    wo_chain.step(len(wo_chain.hops))
    wo_chain.finish()
    for i, (sum_ref, mine, came) in enumerate(
        ((next_sum_ref, next_mine, next_came), (down_sum_ref, down_mine, down_came))
    ):
        loads[i].wait()
        exchanges[i].wait()
        for start in range(0, sum_ref.shape[0], HEAD_SIZE):
            band = slice(start, start + HEAD_SIZE)
            total = mine[band, :].astype(f32) + came[band, :].astype(f32)
            sum_ref[band, :] = total.astype(bf16)


def attention_backward(
    q, ag, kv, lse, delta, kpos, qpos_row, cosine, sine, mine, came, w_out_grad, following,
    following_mine, other_down, mine_down,
):
    n, keys, _ = kv.shape
    rows = q.shape[0]
    chips = sizes()["chip"]
    wo_rows = w_out_grad.shape[0] // 2
    vmem = pl.BlockSpec(memory_space=pltpu.VMEM)
    hbm = pl.BlockSpec(memory_space=pl.ANY)
    return pl.pallas_call(
        functools.partial(attention_back_kernel, n),
        in_specs=[vmem] * 9 + [hbm] * 7,
        out_specs=(vmem,) * 6,
        out_shape=(
            jax.ShapeDtypeStruct((rows, MODEL_WIDTH), bf16),
            jax.ShapeDtypeStruct((keys, 2 * KV_WIDTH), bf16),
            jax.ShapeDtypeStruct((mine.shape[0] // n, mine.shape[1]), f32),
            jax.ShapeDtypeStruct(following.shape, bf16),
            jax.ShapeDtypeStruct(other_down.shape[1:], bf16),
            jax.ShapeDtypeStruct((wo_rows // chips, MODEL_WIDTH), bf16),
        ),
        scratch_shapes=[
            pltpu.VMEM(following.shape, bf16),
            pltpu.VMEM(other_down.shape[1:], bf16),
            pltpu.VMEM(following.shape, bf16),
            pltpu.VMEM(other_down.shape[1:], bf16),
            pltpu.VMEM(mine.shape, bf16),
            pltpu.VMEM(came.shape, bf16),
            pltpu.VMEM((wo_rows, MODEL_WIDTH), bf16),
            pltpu.VMEM((rows, MODEL_WIDTH), f32),
            pltpu.VMEM((KEY_VALUE_HEADS, keys, 2 * HEAD_SIZE), f32),
            pltpu.VMEM((KEY_VALUE_HEADS, n - 1, keys, 2 * HEAD_SIZE), bf16),
            pltpu.VMEM((KEY_VALUE_HEADS, n - 1, keys, 2 * HEAD_SIZE), bf16),
            pltpu.SemaphoreType.DMA((KEY_VALUE_HEADS, n - 1)),
            pltpu.SemaphoreType.DMA((KEY_VALUE_HEADS, n - 1)),
            pltpu.SemaphoreType.DMA((2, 3)),
            pltpu.SemaphoreType.DMA((3,)),
        ]
        + ring_buffers(2, 1, wo_rows, MODEL_WIDTH)
        + [pltpu.VMEM((wo_rows, MODEL_WIDTH), bf16)]
        + ring_buffers(chips, 1, wo_rows // chips, MODEL_WIDTH)
        + ring_buffers(n, 2, mine.shape[0] // n, mine.shape[1]),
        compiler_params=params(collective_id=1, has_side_effects=True),
        cost_estimate=cost(10 * n * rows * keys * MODEL_WIDTH, 4e7, n * rows * keys * QUERY_HEADS),
        name="attention_backward",
    )(
        q, ag, kv, lse, delta, kpos, qpos_row, cosine, sine, mine, came, w_out_grad, following,
        following_mine, other_down, mine_down,
    )


def ring_buffers(count, terms, rows, width):
    sends = count - 1 if terms > 1 else count - 2
    return [
        pltpu.VMEM((sends, rows, width) if sends else (16, HEAD_SIZE), bf16),
        pltpu.VMEM((count - 1, rows, width), bf16),
        pltpu.SemaphoreType.DMA((count - 1,)),
        pltpu.SemaphoreType.DMA((count - 1,)),
    ]


class Chain:
    def __init__(self, rings, stores):
        self.hops = [(r, h) for r in range(len(rings)) for h in range(rings[r].count)]
        self.rings, self.stores, self.done = rings, stores, 0

    def step(self, times=1):
        for _ in range(times):
            if self.done == len(self.hops):
                return
            index, hop = self.hops[self.done]
            self.done += 1
            ring = self.rings[index]
            total = ring.hop(hop)
            if hop == ring.count - 1:
                store = self.stores[index]
                store[...] = total.astype(store.dtype)

    def finish(self):
        assert self.done == len(self.hops)
        for ring in self.rings:
            ring.finish()


FULL_AXES = ("core", "chip", "dp", "ctx")
OWNER_TILE = 384


def owner_rows():
    counts = sizes()
    return MODEL_WIDTH // (2 * counts["chip"] * counts["dp"] * counts["ctx"])


def ordered_in_kernel():
    return owner_rows() % 16 == 0


def store_by_owner(target, a, b):
    share, counts = owner_rows(), sizes()
    for start in range(0, MODEL_WIDTH, OWNER_TILE):
        rows = dot_tn(a[:, start : start + OWNER_TILE], b).astype(bf16)
        if not ordered_in_kernel():
            target[start : start + OWNER_TILE, :] = rows
            continue
        for offset in range(0, OWNER_TILE, share):
            device = (start + offset) // share
            device, core = divmod(device, 2)
            device, chip = divmod(device, counts["chip"])
            dp, ctx = divmod(device, counts["ctx"])
            place = ((core * counts["chip"] + chip) * counts["dp"] + dp) * counts["ctx"] + ctx
            target[place * share : (place + 1) * share, :] = rows[offset : offset + share, :]


def sizes():
    exp = lax.axis_size("exp")
    return {"core": 2, "chip": exp // 2, "dp": lax.axis_size("dp"), "ctx": lax.axis_size("ctx")}


class Total:
    def __init__(self, axis, value, recv, send_sem, recv_sem):
        self.axis, self.value, self.recv = axis, value, recv
        self.send_sem, self.recv_sem = send_sem, recv_sem

    def copy(self, hop):
        source = self.recv.at[hop - 1] if hop else self.value
        return remote(
            source, self.recv.at[hop], self.send_sem.at[hop], self.recv_sem.at[hop], self.axis.next
        )

    def run(self):
        count = self.axis.count
        self.copy(0).start()
        total = self.value[...]
        for hop in range(1, count):
            self.copy(hop - 1).wait_recv()
            total += self.recv[hop - 1]
            if hop < count - 1:
                self.copy(hop).start()
        for hop in range(count - 1):
            self.copy(hop).wait_send()
        self.value[...] = total


GAIN_ROWS = 8


def last_kernel(
    plan, piece_hbm, down_sum_hbm, mine_down_ref, other_down_ref, dql_ref, dkv_ref, normed_ref, wq_hbm,
    wk_hbm, wv_hbm, cos_ref, sin_ref, x_hbm, gain_ref, mg_hbm, ffn_gain_ref, wo_sum_hbm,
    gate_up_ref, down_ref, dx_ref, gains_ref, wq_out, wkv_out, wo_out, wq_grad, wkv_grad, dkvl,
    mg_band, mg_sem, *scratch,
):
    scratch = list(scratch)

    def take(number):
        taken = scratch[:number]
        del scratch[:number]
        return taken

    piece_ref, down_sum_ref, wo_sum_ref, wq_ref, wk_ref, wv_ref, x_ref, load_sem = take(8)
    loads = [
        pltpu.make_async_copy(source, target, load_sem.at[i])
        for i, (source, target) in enumerate(
            (
                (piece_hbm, piece_ref), (down_sum_hbm, down_sum_ref), (wq_hbm, wq_ref),
                (wk_hbm, wk_ref), (wv_hbm, wv_ref), (x_hbm, x_ref), (wo_sum_hbm, wo_sum_ref),
            )
        )
    ]
    axes = {name: Axis(name) for name in FULL_AXES}
    across = axes["dp"].next
    piece = Chain(
        [Ring(axes["ctx"], [piece_ref], gate_up_ref.shape[0], *take(4), piece_hbm)],
        [gate_up_ref],
    )
    came_down, mine_down, down_sem = take(3)
    exchange = remote(
        other_down_ref.at[1], came_down, down_sem.at[0], down_sem.at[1], across
    )
    load_down = pltpu.make_async_copy(mine_down_ref.at[1], mine_down, down_sem.at[2])
    downs = [
        Chain([Ring(axes["ctx"], terms, down_ref.shape[1], *take(4), first)], [down_ref.at[expert]])
        for expert, (terms, first) in enumerate(
            (([down_sum_ref], down_sum_hbm), ([mine_down, came_down], None))
        )
    ]
    chains = []
    for (names, rows), array, out in zip(
        plan, (wq_grad, wkv_grad, wo_sum_ref), (wq_out, wkv_out, wo_out)
    ):
        rings, stores, source = [], [], array
        for name in names:
            rows //= axes[name].count
            if name == "ctx":
                rings.append(Direct(axes[name], source, rows, *take(3)))
            else:
                first = wo_sum_hbm if source is wo_sum_ref else None
                rings.append(Ring(axes[name], [source], rows, *take(4), first))
            source = out if name == names[-1] else take(1)[0]
            stores.append(source)
        chains.append(Chain(rings, stores))
    query, kv, out_chain = chains
    totals = [Total(axes[name], gains_ref, *take(3)) for name in FULL_AXES]
    signal_and_wait([device for axis in axes.values() for device in axis.others()])

    quarter = x_hbm.shape[0] // 4

    def load_mid_grad(part):
        band = slice(part * quarter, (part + 1) * quarter)
        return pltpu.make_async_copy(mg_hbm.at[band, :], mg_band.at[part % 2], mg_sem.at[part])

    piece.step()
    exchange.start()
    out_chain.step()
    downs[0].step()
    for load in loads:
        load.start()
    load_mid_grad(0).start()
    load_mid_grad(1).start()
    load_down.start()
    store_by_owner(wq_grad, normed_ref, dql_ref[...])
    query.step()
    cosine, sine = cos_ref[...], sin_ref[...]
    for head in range(KEY_VALUE_HEADS):
        span = slice(head * HEAD_SIZE, (head + 1) * HEAD_SIZE)
        dkvl[:, span] = rotate_back(dkv_ref[:, span].astype(f32), cosine, sine).astype(bf16)
    dkvl[:, KV_WIDTH:] = dkv_ref[:, KV_WIDTH:]
    store_by_owner(wkv_grad, normed_ref, dkvl[...])
    query.step(2)
    kv.step()
    for load in loads:
        load.wait()
    piece.step()
    downs[0].step()
    dgain = jnp.zeros((1, MODEL_WIDTH), f32)
    for part in range(4):
        band = slice(part * quarter, (part + 1) * quarter)
        grad = dot_nt(dql_ref[band, :], wq_ref[...])
        grad += dot_nt(dkvl[band, :KV_WIDTH], wk_ref[...])
        grad += dot_nt(dkvl[band, KV_WIDTH:], wv_ref[...])
        x = x_ref[band, :].astype(f32)
        r = lax.rsqrt(jnp.mean(x * x, axis=-1, keepdims=True) + epsilon)
        v = grad * gain_ref[...]
        inner = jnp.mean(v * x, axis=-1, keepdims=True)
        dgain += jnp.sum(grad * x * r, axis=0, keepdims=True)
        load_mid_grad(part).wait()
        mid_grad = mg_band[part % 2]
        dx_ref[band, :] = (mid_grad + r * v - x * (r * r * r * inner)).astype(bf16)
        if part < 2:
            load_mid_grad(part + 2).start()
        if part == 1:
            kv.step()
    gains_ref[0:1, :] = dgain
    gains_ref[1:2, :] = ffn_gain_ref[...]
    gains_ref[2:, :] = jnp.zeros((GAIN_ROWS - 2, MODEL_WIDTH), f32)
    out_chain.step(2)
    totals[0].run()
    totals[1].run()
    totals[2].run()
    piece.step()
    downs[0].step()
    query.step(2)
    kv.step()
    load_down.wait()
    exchange.wait_recv()
    downs[1].step()
    out_chain.step()
    totals[3].run()
    kv.step(2)
    query.step(2)
    out_chain.step()
    downs[1].step()
    kv.step(2)
    piece.step()
    downs[0].step()
    query.step()
    downs[1].step()
    kv.step()
    everything = [query, kv, downs[1], downs[0], out_chain, piece]
    while any(chain.done < len(chain.hops) for chain in everything):
        for chain in everything:
            chain.step()
    for chain in everything:
        chain.finish()
    exchange.wait_send()


def last_part(
    piece, down_sum, mine_down, other_down, dql, dkv, normed, wq, wk, wv, cosine, sine, x, gain,
    mg, ffn_gain_part, wo_sum,
):
    counts = sizes()
    n = counts["ctx"]
    full = FULL_AXES if ordered_in_kernel() else FULL_AXES[:3]
    widths = (MODEL_WIDTH, 2 * KV_WIDTH, MODEL_WIDTH)
    plan = [(full, MODEL_WIDTH), (full, MODEL_WIDTH), (full[2:], wo_sum.shape[0])]
    share, down_share = piece.shape[0] // n, mine_down.shape[1] // n
    shapes = [
        jax.ShapeDtypeStruct((share, 2 * FF), f32),
        jax.ShapeDtypeStruct((EXP_DEV, down_share, mine_down.shape[2]), f32),
        jax.ShapeDtypeStruct(x.shape, bf16),
        jax.ShapeDtypeStruct((GAIN_ROWS, MODEL_WIDTH), f32),
    ]
    scratch = [
        pltpu.VMEM((MODEL_WIDTH, MODEL_WIDTH), bf16),
        pltpu.VMEM((MODEL_WIDTH, 2 * KV_WIDTH), bf16),
        pltpu.VMEM((x.shape[0], 2 * KV_WIDTH), bf16),
        pltpu.VMEM((2, x.shape[0] // 4, MODEL_WIDTH), f32),
        pltpu.SemaphoreType.DMA((4,)),
    ]
    scratch += [
        pltpu.VMEM(a.shape, bf16) for a in (piece, down_sum, wo_sum, wq, wk, wv, x)
    ]
    scratch.append(pltpu.SemaphoreType.DMA((7,)))
    scratch += ring_buffers(n, 1, share, 2 * FF)
    scratch += [pltpu.VMEM(mine_down.shape[1:], bf16)] * 2 + [pltpu.SemaphoreType.DMA((3,))]
    for terms in (1, 2):
        scratch += ring_buffers(n, terms, down_share, mine_down.shape[2])
    for (names, rows), width in zip(plan, widths):
        for name in names:
            rows //= counts[name]
            scratch += ring_buffers(counts[name], 1, rows, width)[name == "ctx" :]
            if name != names[-1]:
                scratch.append(pltpu.VMEM((rows, width), bf16))
        shapes.append(jax.ShapeDtypeStruct((rows, width), f32 if "ctx" in names else bf16))
    for name in FULL_AXES:
        hops = counts[name] - 1
        scratch += [
            pltpu.VMEM((hops, GAIN_ROWS, MODEL_WIDTH), f32),
            pltpu.SemaphoreType.DMA((hops,)),
            pltpu.SemaphoreType.DMA((hops,)),
        ]
    vmem, hbm = pl.BlockSpec(memory_space=pltpu.VMEM), pl.BlockSpec(memory_space=pl.ANY)
    gate_up, down, dx, gains, *attention = pl.pallas_call(
        functools.partial(last_kernel, plan),
        in_specs=[hbm] * 4 + [vmem] * 3 + [hbm] * 3 + [vmem] * 2 + [hbm, vmem, hbm, vmem, hbm],
        out_specs=(vmem,) * 7,
        out_shape=tuple(shapes),
        scratch_shapes=scratch,
        compiler_params=params(collective_id=2, has_side_effects=True),
        cost_estimate=cost(1e10, 4e7),
        name="last_part",
    )(
        piece, down_sum, mine_down, other_down, dql, dkv, normed, wq, wk, wv, cosine, sine, x, gain,
        mg, ffn_gain_part, wo_sum,
    )
    if "ctx" not in full:
        attention = [
            scatter_axis(a.reshape(n, a.shape[0] // n, a.shape[1]), "ctx").astype(f32)
            for a in attention
        ]
    return gate_up, down, dx, gains, attention


def shifted(value, axis, steps):
    count = lax.axis_size(axis)
    return lax.ppermute(value, axis, [(i, (i + steps) % count) for i in range(count)])


def chip_shift(value, steps):
    count = lax.axis_size("exp")
    return lax.ppermute(value, "exp", [(i, (i + 2 * steps) % count) for i in range(count)])


def ring_part(parts, index, count, step, axis=0):
    return lax.dynamic_index_in_dim(parts, (index - 1 - step) % count, axis, keepdims=False)


def add_low(a, b):
    return (a.astype(f32) + b.astype(f32)).astype(bf16)


def ring_scatter(parts, shift, index, count, axis=0):
    total = ring_part(parts, index, count, 0, axis)
    for step in range(1, count):
        total = add_low(shift(total), ring_part(parts, index, count, step, axis))
    return total


def by_owner(array, axis):
    dp, ctx, exp = (lax.axis_size(a) for a in ("dp", "ctx", "exp"))
    size = array.shape[axis]
    before, after = array.shape[:axis], array.shape[axis + 1 :]
    parts = array.reshape(*before, dp, ctx, exp // 2, 2, size // (dp * ctx * exp), *after)
    order = list(range(axis)) + [axis + i for i in (3, 2, 0, 1, 4)]
    order += list(range(axis + 5, parts.ndim))
    return jnp.transpose(parts, order).reshape(array.shape)


def scatter_axis(parts, axis):
    return ring_scatter(
        parts, lambda v: shifted(v, axis, 1), lax.axis_index(axis), lax.axis_size(axis)
    )


def tie(*values):
    return lax.optimization_barrier(values)


def per_device(
    tokens, attn_gain, w_query, key_matrix, value_matrix, w_out, ffn_gain, expert_gate_up,
    expert_down, expert_ids, gate_weights, span_order, out_grad,
):
    ctx_size, exp_size = lax.axis_size("ctx"), lax.axis_size("exp")
    ctx_here, exp_here = lax.axis_index("ctx"), lax.axis_index("exp")
    experts = EXP_DEV * exp_size
    x, g = tokens[0], out_grad[0]
    rows = x.shape[0]
    capacity = rows * TOPK * 5 // (4 * experts)
    gain_one, gain_two = attn_gain[None, :], ffn_gain[None, :]
    offsets = jnp.arange(HALF, dtype=jnp.int32)

    def device_positions(device):
        pair = lax.dynamic_slice_in_dim(span_order[0], 2 * device, 2, 0)
        return (pair[:, None] * HALF + offsets[None, :]).reshape(-1)

    sources = [(ctx_here - s) % ctx_size for s in range(ctx_size)]
    key_positions = [device_positions(s) for s in sources]
    positions = key_positions[0]
    exponent = jnp.arange(HEAD_SIZE // 2, dtype=f32) * (-2.0 / HEAD_SIZE)
    frequency = jnp.power(f32(rope_base), exponent)
    angles = positions.astype(f32)[:, None] * frequency[None, :]
    cosine, sine = jnp.cos(angles), jnp.sin(angles)
    cosine = jnp.concatenate([cosine, cosine], axis=1)
    sine = jnp.concatenate([-sine, sine], axis=1)

    kpos_rows = jnp.stack(key_positions)[:, None, :]
    normed, q, kv, att, att_low, lse, mid, nf, g_all, *routing = forward_to_experts(
        x, gain_one, key_matrix, value_matrix, cosine, sine, positions[:, None],
        kpos_rows, gain_two, w_query, w_out, g, expert_ids[0].T,
        gate_weights[0].T,
    )

    dx_chip, y_chip, dx_far, y_far, *kept, _ = expert_blocks(
        capacity, *routing, nf, g_all, expert_gate_up, expert_down
    )
    slot_rows, hidden, slot_grad, projected_grad = (
        a.reshape(EXP_DEV, exp_size * capacity, a.shape[-1]) for a in kept
    )
    nf_grad_terms = [dx_chip] + [
        chip_shift(dx_far[s - 1], -s) for s in range(1, exp_size // 2)
    ]
    dp_size, dp_here = lax.axis_size("dp"), lax.axis_index("dp")
    theirs = weight_grad(
        0, 1, (dp_here - 1) % dp_size, MODEL_WIDTH // dp_size, slot_rows, projected_grad
    )[0]
    if not ordered_in_kernel():
        normed, att_low = by_owner(normed, 1), by_owner(att_low, 1)
    slot_rows, theirs = tie(slot_rows, theirs)
    came = shifted(theirs, "dp", 1)
    theirs_next, mine, mine_next, other_down, mine_down = other_weight_grads(
        dp_here, dp_size, slot_rows, projected_grad, hidden, slot_grad
    )
    nf_grad_terms, mine, y_far = tie(nf_grad_terms, mine, y_far)

    mid_grad, att_grad, delta, ffn_gain_part, w_out_grad = middle_backward(
        nf_grad_terms, mid, g, gain_two, w_out, att, att_low
    )
    att_grad, came = tie(att_grad, came)
    y_terms = [y_chip] + [chip_shift(y_far[s - 1], -s) for s in range(1, exp_size // 2)]

    dql, dkv, gate_up_first, gate_up_next, down_sum, w_out_sum = attention_backward(
        q, att_grad, kv, lse, delta, kpos_rows, positions[None, :],
        cosine, sine, mine, came, w_out_grad, theirs_next, mine_next, other_down, mine_down,
    )
    gate_up_second, down_share, tokens_grad, gains, attention = last_part(
        gate_up_next, down_sum, mine_down, other_down, dql, dkv, normed, w_query, key_matrix,
        value_matrix, cosine, sine, x, gain_one, mid_grad, ffn_gain_part, w_out_sum,
    )
    w_query_share, w_kv_share, w_out_share = attention
    layer_output = mid
    for term in y_terms:
        layer_output = layer_output + term.astype(f32)
    layer_output = layer_output.astype(bf16)
    owner = (lax.axis_index("dp") * ctx_size + ctx_here) * exp_size + exp_here
    gain_share = MODEL_WIDTH // (dp_size * ctx_size * exp_size)
    gains = lax.dynamic_slice_in_dim(gains, owner * gain_share, gain_share, 1)
    return (
        layer_output[None],
        tokens_grad[None],
        gains[0],
        w_query_share,
        w_kv_share[:, :KV_WIDTH],
        w_kv_share[:, KV_WIDTH:],
        w_out_share,
        gains[1],
        jnp.stack([gate_up_first, gate_up_second]),
        down_share,
    )


def solution(mesh):
    by_row = P(("dp", "exp"), "ctx", None)
    share = P(("dp", "ctx", "exp"))
    share_rows = P(("dp", "ctx", "exp"), None)
    return jax.shard_map(
        per_device,
        mesh=mesh,
        in_specs=(
            by_row, P(), P(), P(), P(), P(), P(), P("exp", None, None), P("exp", None, None),
            by_row, by_row, P(("dp", "exp"), None), by_row,
        ),
        out_specs=(
            by_row, by_row, share, share_rows, share_rows, share_rows, share_rows, share,
            P("exp", ("dp", "ctx"), None), P("exp", ("dp", "ctx"), None),
        ),
        check_vma=False,
    )
```

profile of v0, /device:TPU:0, one launch (start us, length us, event | category | flops | bytes accessed | tf_op | source)
XLA Modules:
  0.0 450.3 jit_solution(14632561647214156560)
XLA Ops:
  0.8 0.9 fusion.6
  1.7 0.1 fusion.2
  1.7 1.0 fusion.1
  2.7 0.8 pad_maximum_fusion.1.cos_ref
  3.6 0.9 copy.30
  4.4 0.1 add_bitcast_fusion.1
  4.6 0.6 copy.26.kpos_ref
  5.2 1.3 broadcast_in_dim.10.gain_ref
  6.5 1.3 broadcast_in_dim.12.ffn_gain_ref.refs_4_
  7.8 0.8 pad_maximum_fusion.2.sin_ref
  8.6 70.0 %forward_to_experts.1 = (bf16[512,1536]{1,0:T(8,128)(2,1)}, bf16[512,1536]{1,0:T(8,128)(2,1)}, bf16[4,512,512]{2,1,0:T(8,128)(2,1)}, f32[512,1536]{1,0:T(8,128)}...) custom-call(bf16[512,1536]{1,0:T(8,128)(2,1)} %bitcast.66, ...), custom_call_target="tpu_custom_call" | custom-call | flops 390070272 | bytes 1250000 | tf_op jit(solution)/shard_map/forward_to_experts/pallas_call | solution.py:260
  78.7 88.0 %expert_blocks.1 = (bf16[512,1536]{1,0:T(8,128)(2,1)}, bf16[512,1536]{1,0:T(8,128)(2,1)}, bf16[1,512,1536]{2,1,0:T(8,128)(2,1)}, bf16[1,512,1536]{2,1,0:T(8,128)...) custom-call(f32[4,512,128]{2,1,0:T(8,128)} %get-tuple-element.61.pla, ...), custom_call_target="tpu_custom_call" | custom-call | flops 2202009600 | bytes 1875000 | tf_op jit(solution)/shard_map/expert_blocks/pallas_call | solution.py:461
  166.7 6.9 %weight_grad.1 = bf16[1,768,1536]{2,1,0:T(8,128)(2,1)} custom-call(s32[1]{0:T(128)} %bitcast.14.chunk_ref, bf16[2,1280,1536]{2,1,0:T(8,128)(2,1)} %bitcast.59, bf16[2,1280,1536]{2,1,0:T(8,128)(2,1)} %bitcast.61), custom_call_target="tpu_custom_call" | custom-call | flops 94371840 | bytes 625000 | tf_op jit(solution)/shard_map/weight_grad/pallas_call | solution.py:507
  173.6 1.5 collective-permute-start.2
  175.1 1.0 collective-permute-start
  176.1 27.7 %other_weight_grads.1 = (bf16[768,1536]{1,0:T(8,128)(2,1)}, bf16[768,1536]{1,0:T(8,128)(2,1)}, bf16[768,1536]{1,0:T(8,128)(2,1)}, bf16[2,384,1536]{2,1,0:T(8,128)(2,1)}, bf16[2,384,1536]{2,1,0:T(8,128)(2,1)}) custom-call(s32[1]{0:T(128)} %bitcast.12.dp_ref, bf16[2,1280,1536]{2,1,0:T(8,128)(2,1)} %bitcast.60, bf16[2,1280,1536]{2,1,0:T(8,128)(2,1)} %bitcast.62, ...), custom_call_target="tpu_custom_call" | custom-call | flops 471859200 | bytes 1562500 | tf_op jit(solution)/shard_map/other_weight_grads/pallas_call | solution.py:572
  203.8 8.5 %collective-permute-done.refs_1_ = bf16[512,1536]{1,0:T(8,128)(2,1)} collective-permute-done((bf16[512,1536]{1,0:T(8,128)(2,1)}, bf16[512,1536]{1,0:T(8,128)(2,1)}, u32[]{:S(2)}, u32[]{:S(2)}) %collective-permute-start) | collective-permute-done | bytes 1572896 | tf_op jit(solution)/shard_map/ppermute | solution.py:1249
  212.3 1.0 collective-permute-start.1
  213.3 14.5 %middle_backward.1 = (f32[512,1536]{1,0:T(8,128)}, bf16[512,1536]{1,0:T(8,128)(2,1)}, f32[16,512]{1,0:T(8,128)}, f32[1,1536]{1,0:T(1,128)}, bf16[1536,1536]{1,0:T(8,128)(2,1)}) custom-call(bf16[512,1536]{1,0:T(8,128)(2,1)} %get-tuple-element.77.refs_0_, bf16[512,1536]{1,0:T(8,128)(2,1)} %collective-permute-done.refs_1_, ...), custom_call_target="tpu_custom_call" | custom-call | flops 150994944 | bytes 937500 | tf_op jit(solution)/shard_map/middle_backward/pallas_call | solution.py:631
  227.9 0.1 collective-permute-done.2.came_hbm
  227.9 87.4 %attention_backward.1 = (bf16[512,1536]{1,0:T(8,128)(2,1)}, bf16[512,512]{1,0:T(8,128)(2,1)}, f32[192,1536]{1,0:T(8,128)}, bf16[768,1536]{1,0:T(8,128)(2,1)}, bf...) custom-call(bf16[512,1536]{1,0:T(8,128)(2,1)} %get-tuple-element.76.q_ref, ...), custom_call_target="tpu_custom_call" | custom-call | flops 503316480 | bytes 1250000 | tf_op jit(solution)/shard_map/attention_backward/pallas_call | solution.py:897
  315.3 121.6 %last_part.1 = (f32[192,1536]{1,0:T(8,128)}, f32[2,96,1536]{2,1,0:T(8,128)}, bf16[512,1536]{1,0:T(8,128)(2,1)}, f32[8,1536]{1,0:T(8,128)}, f32[48,1536]{1,0:T(8,...) custom-call(bf16[768,1536]{1,0:T(8,128)(2,1)} %get-tuple-element.94.piece_hbm, ...), custom_call_target="tpu_custom_call" | custom-call | flops 312500000 | bytes 1250000 | tf_op jit(solution)/shard_map/last_part/pallas_call | solution.py:1221
  436.9 0.8 constant_dynamic-slice_fusion
  437.7 0.5 slice_bitcast_fusion
  438.2 1.5 fusion.11
  439.7 3.3 pad_maximum_fusion
  443.0 0.2 copy-done.2
  443.2 3.3 fusion
  446.5 1.1 copy.39
  447.6 0.7 copy.40
  448.3 0.7 copy.41
  449.1 1.0 copy.42
  (21 shorter events, 0.1 us)
Async XLA Ops:
  3.6 75.1 %copy-start.6 = (s32[1,1,2,256]{3,1,2,0:T(1,128)}, s32[1,1,2,256]{3,1,2,0:T(1,128)S(1)}, u32[]{:S(2)}) copy-start(s32[1,1,2,256]{3,1,2,0:T(1,128)S(1)} %copy.29) | copy-start | bytes 6148
  173.6 54.3 %collective-permute-start.2 = (bf16[768,1536]{1,0:T(8,128)(2,1)}, bf16[768,1536]{1,0:T(8,128)(2,1)}, u32[]{:S(2)}, u32[]{:S(2)}) collective-permute-start(bf16[768,1536]{1,0:T(8,128)(2,1)} %bitcast.69), channel_id=1, source_target_pairs={{0,16},{16,0},{1,17},{17,1},{2,18},{18,2},{3,19},{19,3},{4,20},{20... | collective-permute-start | bytes 7077896 | tf_op jit(solution)/shard_map/ppermute | solution.py:1244
  175.1 37.2 %collective-permute-start = (bf16[512,1536]{1,0:T(8,128)(2,1)}, bf16[512,1536]{1,0:T(8,128)(2,1)}, u32[]{:S(2)}, u32[]{:S(2)}) collective-permute-start(bf16[512,1536]{1,0:T(8,128)(2,1)} %bitcast.84), channel_id=1, source_target_pairs={{0,2},{1,3},{2,0},{3,1},{4,6},{5,7},{6,4},{7,5},{8,10},{9,11},{10,... | collective-permute-start | bytes 4718600 | tf_op jit(solution)/shard_map/ppermute | solution.py:1249
  212.3 230.7 %collective-permute-start.1 = (bf16[512,1536]{1,0:T(8,128)(2,1)}, bf16[512,1536]{1,0:T(8,128)(2,1)}, u32[]{:S(2)}, u32[]{:S(2)}) collective-permute-start(bf16[512,1536]{1,0:T(8,128)(2,1)} %bitcast.83), channel_id=1, source_target_pairs={{0,2},{1,3},{2,0},{3,1},{4,6},{5,7},{6,4},{7,5},{8,10},{9,11},{10,... | collective-permute-start | bytes 4718600 | tf_op jit(solution)/shard_map/ppermute | solution.py:1249
  439.7 3.3 copy-start
  439.7 3.5 copy-start.2
  443.2 3.3 copy-start.1
  446.5 1.2 copy-start.5
  446.5 1.9 copy-start.4
  446.5 2.6 copy-start.3
where the time goes:
time: 459 us; the launch traced here: 450 us
  Pallas kernels  416 us (91%)
  local copies, waits for them, and re-layouts  10.6 us (2%)
  other arithmetic  10.4 us (2%)
  waiting for transfers between devices  8.55 us (2%)
    pallas_call x1, Pallas kernels, last_part(): pl.pallas_call(functools.partial(last_kernel, plan), in_specs=[hbm] * 4 +...  122 us
    pallas_call x1, Pallas kernels, expert_blocks(): pl.pallas_call(expert_kernel, grid=(blocks, EXP_DEV), in_specs=[pl.BlockS...  88 us
    pallas_call x1, Pallas kernels, attention_backward(): pl.pallas_call(functools.partial(attention_back_kernel, n), in_specs=[vme...  87.4 us
    pallas_call x1, Pallas kernels, forward_to_experts(): pl.pallas_call(functools.partial(forward_kernel, n), in_specs=[vmem] * 9...  70 us
    pallas_call x1, Pallas kernels, other_weight_grads(): pl.pallas_call(other_weight_grads_kernel, grid_spec=pltpu.PrefetchScalarG...  27.7 us
    pallas_call x1, Pallas kernels, middle_backward(): pl.pallas_call(middle_kernel, out_shape=(jax.ShapeDtypeStruct((rows, MODE...  14.5 us
  transfers between devices with their start and end apart: 3, of which 2 were waited for; matrix products, arithmetic and copies ran while one was open for 1% of the time, Pallas kernels for 56%

commit v1 on v0

--- a/solution.py
+++ b/solution.py
@@ -52,7 +52,7 @@
 
 
 def cost(flops, size, exps=0):
-    return pl.CostEstimate(flops=int(flops) // 32, bytes_accessed=int(size) // 32, transcendentals=int(exps) // 32)
+    return pl.CostEstimate(flops=int(flops), bytes_accessed=int(size), transcendentals=int(exps))
 
 
 def whole(shape):
@@ -169,7 +169,7 @@
     rows = x_ref.shape[0]
     x = x_ref[...].astype(f32)
     r = lax.rsqrt(jnp.mean(x * x, axis=-1, keepdims=True) + epsilon)
-    normed_ref[...] = (x * r * gain_ref[...]).astype(bf16)
+    normed_ref[...] = (x * r * gain_ref[...][None, :]).astype(bf16)
     normed = normed_ref[...]
     cosine, sine = cos_ref[...], sin_ref[...]
     keys = dot(normed, wk_ref[...])
@@ -240,7 +240,7 @@
         mid = x_ref[band, :].astype(f32) + dot(att_low_ref[band, :], wo_ref[...])
         mid_ref[band, :] = mid
         r = lax.rsqrt(jnp.mean(mid * mid, axis=-1, keepdims=True) + epsilon)
-        nf_ref[band, :] = (mid * r * ffn_gain_ref[...]).astype(bf16)
+        nf_ref[band, :] = (mid * r * ffn_gain_ref[...][None, :]).astype(bf16)
     for step in range(n - 1):
         pass_on(step).wait_send()
     for gather in gathers:
@@ -606,7 +606,7 @@
             nf_grad += other[band, :].astype(f32)
         mid = mid_ref[band, :]
         r = lax.rsqrt(jnp.mean(mid * mid, axis=-1, keepdims=True) + epsilon)
-        u = nf_grad * gain_ref[...]
+        u = nf_grad * gain_ref[...][None, :]
         inner = jnp.mean(u * mid, axis=-1, keepdims=True)
         grad = g_ref[band, :].astype(f32) + r * u - mid * (r * r * r * inner)
         dgain += jnp.sum(nf_grad * mid * r, axis=0, keepdims=True)
@@ -1005,7 +1005,7 @@
 
 class Total:
     def __init__(self, axis, value, recv, send_sem, recv_sem):
-        self.axis, self.value, self.recv = axis, value, recv
+        self.axis, self.count, self.value, self.recv = axis, axis.count, value, recv
         self.send_sem, self.recv_sem = send_sem, recv_sem
 
     def copy(self, hop):
@@ -1014,18 +1014,22 @@
             source, self.recv.at[hop], self.send_sem.at[hop], self.recv_sem.at[hop], self.axis.next
         )
 
-    def run(self):
-        count = self.axis.count
-        self.copy(0).start()
-        total = self.value[...]
-        for hop in range(1, count):
-            self.copy(hop - 1).wait_recv()
-            total += self.recv[hop - 1]
-            if hop < count - 1:
-                self.copy(hop).start()
-        for hop in range(count - 1):
-            self.copy(hop).wait_send()
-        self.value[...] = total
+    def hop(self, hop):
+        if hop == 0:
+            self.copy(0).start()
+            self.total = self.value[...]
+            return None
+        self.copy(hop - 1).wait_recv()
+        self.total += self.recv[hop - 1]
+        if hop < self.count - 1:
+            self.copy(hop).start()
+        else:
+            for sent in range(hop):
+                self.copy(sent).wait_send()
+        return self.total
+
+    def finish(self):
+        pass
 
 
 GAIN_ROWS = 8
@@ -1087,7 +1091,9 @@
             stores.append(source)
         chains.append(Chain(rings, stores))
     query, kv, out_chain = chains
-    totals = [Total(axes[name], gains_ref, *take(3)) for name in FULL_AXES]
+    gains = Chain(
+        [Total(axes[name], gains_ref, *take(3)) for name in FULL_AXES], [gains_ref] * len(FULL_AXES)
+    )
     signal_and_wait([device for axis in axes.values() for device in axis.others()])
 
     quarter = x_hbm.shape[0] // 4
@@ -1127,7 +1133,7 @@
         grad += dot_nt(dkvl[band, KV_WIDTH:], wv_ref[...])
         x = x_ref[band, :].astype(f32)
         r = lax.rsqrt(jnp.mean(x * x, axis=-1, keepdims=True) + epsilon)
-        v = grad * gain_ref[...]
+        v = grad * gain_ref[...][None, :]
         inner = jnp.mean(v * x, axis=-1, keepdims=True)
         dgain += jnp.sum(grad * x * r, axis=0, keepdims=True)
         load_mid_grad(part).wait()
@@ -1140,30 +1146,31 @@
     gains_ref[0:1, :] = dgain
     gains_ref[1:2, :] = ffn_gain_ref[...]
     gains_ref[2:, :] = jnp.zeros((GAIN_ROWS - 2, MODEL_WIDTH), f32)
+    gains.step()
     out_chain.step(2)
-    totals[0].run()
-    totals[1].run()
-    totals[2].run()
     piece.step()
+    gains.step(2)
     downs[0].step()
     query.step(2)
     kv.step()
     load_down.wait()
     exchange.wait_recv()
+    gains.step(2)
     downs[1].step()
     out_chain.step()
-    totals[3].run()
     kv.step(2)
     query.step(2)
+    gains.step(2)
     out_chain.step()
     downs[1].step()
     kv.step(2)
     piece.step()
+    gains.step()
     downs[0].step()
     query.step()
     downs[1].step()
     kv.step()
-    everything = [query, kv, downs[1], downs[0], out_chain, piece]
+    everything = [query, kv, downs[1], downs[0], out_chain, piece, gains]
     while any(chain.done < len(chain.hops) for chain in everything):
         for chain in everything:
             chain.step()
@@ -1294,7 +1301,6 @@
     x, g = tokens[0], out_grad[0]
     rows = x.shape[0]
     capacity = rows * TOPK * 5 // (4 * experts)
-    gain_one, gain_two = attn_gain[None, :], ffn_gain[None, :]
     offsets = jnp.arange(HALF, dtype=jnp.int32)
 
     def device_positions(device):
@@ -1313,8 +1319,8 @@
 
     kpos_rows = jnp.stack(key_positions)[:, None, :]
     normed, q, kv, att, att_low, lse, mid, nf, g_all, *routing = forward_to_experts(
-        x, gain_one, key_matrix, value_matrix, cosine, sine, positions[:, None],
-        kpos_rows, gain_two, w_query, w_out, g, expert_ids[0].T,
+        x, attn_gain, key_matrix, value_matrix, cosine, sine, positions[:, None],
+        kpos_rows, ffn_gain, w_query, w_out, g, expert_ids[0].T,
         gate_weights[0].T,
     )
 
@@ -1341,7 +1347,7 @@
     nf_grad_terms, mine, y_far = tie(nf_grad_terms, mine, y_far)
 
     mid_grad, att_grad, delta, ffn_gain_part, w_out_grad = middle_backward(
-        nf_grad_terms, mid, g, gain_two, w_out, att, att_low
+        nf_grad_terms, mid, g, ffn_gain, w_out, att, att_low
     )
     att_grad, came = tie(att_grad, came)
     y_terms = [y_chip] + [chip_shift(y_far[s - 1], -s) for s in range(1, exp_size // 2)]
@@ -1352,7 +1358,7 @@
     )
     gate_up_second, down_share, tokens_grad, gains, attention = last_part(
         gate_up_next, down_sum, mine_down, other_down, dql, dkv, normed, w_query, key_matrix,
-        value_matrix, cosine, sine, x, gain_one, mid_grad, ffn_gain_part, w_out_sum,
+        value_matrix, cosine, sine, x, attn_gain, mid_grad, ffn_gain_part, w_out_sum,
     )
     w_query_share, w_kv_share, w_out_share = attention
     layer_output = mid

time: 459 us -> 455 us (level)
  no operation moved by 1% of the time
where the time goes in v1:
time: 455 us; the launch traced here: 450 us
  Pallas kernels  419 us (92%)
  other arithmetic  10.4 us (2%)
  waiting for transfers between devices  8.55 us (2%)
  local copies, waits for them, and re-layouts  8.03 us (2%)
    pallas_call x1, Pallas kernels, last_part(): pl.pallas_call(functools.partial(last_kernel, plan), in_specs=[hbm] * 4 +...  124 us
    pallas_call x1, Pallas kernels, expert_blocks(): pl.pallas_call(expert_kernel, grid=(blocks, EXP_DEV), in_specs=[pl.BlockS...  88 us
    pallas_call x1, Pallas kernels, attention_backward(): pl.pallas_call(functools.partial(attention_back_kernel, n), in_specs=[vme...  87.4 us
    pallas_call x1, Pallas kernels, forward_to_experts(): pl.pallas_call(functools.partial(forward_kernel, n), in_specs=[vmem] * 9...  70 us
    pallas_call x1, Pallas kernels, other_weight_grads(): pl.pallas_call(other_weight_grads_kernel, grid_spec=pltpu.PrefetchScalarG...  27.7 us
    pallas_call x1, Pallas kernels, middle_backward(): pl.pallas_call(middle_kernel, out_shape=(jax.ShapeDtypeStruct((rows, MODE...  14.5 us
  transfers between devices with their start and end apart: 3, of which 2 were waited for; matrix products, arithmetic and copies ran while one was open for 1% of the time, Pallas kernels for 56%

profile of v1, /device:TPU:0, one launch (start us, length us, event | category | flops | bytes accessed | tf_op | source)
XLA Modules:
  0.0 450.2 jit_solution(10981146960012873303)
XLA Ops:
  0.8 0.9 fusion.6
  1.7 0.1 fusion.2
  1.7 1.0 fusion.1
  2.7 0.8 pad_maximum_fusion.1.cos_ref
  3.6 0.9 copy.30
  4.4 0.1 add_bitcast_fusion.1
  4.6 0.6 copy.26.kpos_ref
  5.2 0.8 pad_maximum_fusion.2.sin_ref
  6.0 70.0 %forward_to_experts.1 = (bf16[512,1536]{1,0:T(8,128)(2,1)}, bf16[512,1536]{1,0:T(8,128)(2,1)}, bf16[4,512,512]{2,1,0:T(8,128)(2,1)}, f32[512,1536]{1,0:T(8,128)}...) custom-call(bf16[512,1536]{1,0:T(8,128)(2,1)} %bitcast.77, ...), custom_call_target="tpu_custom_call" | custom-call | flops 12482248704 | bytes 40000000 | tf_op jit(solution)/shard_map/forward_to_experts/pallas_call | solution.py:260
  76.1 88.0 %expert_blocks.1 = (bf16[512,1536]{1,0:T(8,128)(2,1)}, bf16[512,1536]{1,0:T(8,128)(2,1)}, bf16[1,512,1536]{2,1,0:T(8,128)(2,1)}, bf16[1,512,1536]{2,1,0:T(8,128)...) custom-call(f32[4,512,128]{2,1,0:T(8,128)} %get-tuple-element.61.pla, ...), custom_call_target="tpu_custom_call" | custom-call | flops 70464307200 | bytes 60000000 | tf_op jit(solution)/shard_map/expert_blocks/pallas_call | solution.py:461
  164.1 6.9 %weight_grad.1 = bf16[1,768,1536]{2,1,0:T(8,128)(2,1)} custom-call(s32[1]{0:T(128)} %bitcast.14.chunk_ref, bf16[2,1280,1536]{2,1,0:T(8,128)(2,1)} %bitcast.59, bf16[2,1280,1536]{2,1,0:T(8,128)(2,1)} %bitcast.61), custom_call_target="tpu_custom_call" | custom-call | flops 3019898880 | bytes 20000000 | tf_op jit(solution)/shard_map/weight_grad/pallas_call | solution.py:507
  171.0 1.5 collective-permute-start.2
  172.5 1.0 collective-permute-start
  173.5 27.7 %other_weight_grads.1 = (bf16[768,1536]{1,0:T(8,128)(2,1)}, bf16[768,1536]{1,0:T(8,128)(2,1)}, bf16[768,1536]{1,0:T(8,128)(2,1)}, bf16[2,384,1536]{2,1,0:T(8,128)(2,1)}, bf16[2,384,1536]{2,1,0:T(8,128)(2,1)}) custom-call(s32[1]{0:T(128)} %bitcast.12.dp_ref, bf16[2,1280,1536]{2,1,0:T(8,128)(2,1)} %bitcast.60, bf16[2,1280,1536]{2,1,0:T(8,128)(2,1)} %bitcast.62, ...), custom_call_target="tpu_custom_call" | custom-call | flops 15099494400 | bytes 50000000 | tf_op jit(solution)/shard_map/other_weight_grads/pallas_call | solution.py:572
  201.2 8.5 %collective-permute-done.refs_1_ = bf16[512,1536]{1,0:T(8,128)(2,1)} collective-permute-done((bf16[512,1536]{1,0:T(8,128)(2,1)}, bf16[512,1536]{1,0:T(8,128)(2,1)}, u32[]{:S(2)}, u32[]{:S(2)}) %collective-permute-start) | collective-permute-done | bytes 1572896 | tf_op jit(solution)/shard_map/ppermute | solution.py:1256
  209.7 1.0 collective-permute-start.1
  210.7 14.5 %middle_backward.1 = (f32[512,1536]{1,0:T(8,128)}, bf16[512,1536]{1,0:T(8,128)(2,1)}, f32[16,512]{1,0:T(8,128)}, f32[1,1536]{1,0:T(1,128)}, bf16[1536,1536]{1,0:T(8,128)(2,1)}) custom-call(bf16[512,1536]{1,0:T(8,128)(2,1)} %get-tuple-element.77.refs_0_, bf16[512,1536]{1,0:T(8,128)(2,1)} %collective-permute-done.refs_1_, ...), custom_call_target="tpu_custom_call" | custom-call | flops 4831838208 | bytes 30000000 | tf_op jit(solution)/shard_map/middle_backward/pallas_call | solution.py:631
  225.3 0.1 collective-permute-done.2.came_hbm
  225.4 87.4 %attention_backward.1 = (bf16[512,1536]{1,0:T(8,128)(2,1)}, bf16[512,512]{1,0:T(8,128)(2,1)}, f32[192,1536]{1,0:T(8,128)}, bf16[768,1536]{1,0:T(8,128)(2,1)}, bf...) custom-call(bf16[512,1536]{1,0:T(8,128)(2,1)} %get-tuple-element.76.q_ref, ...), custom_call_target="tpu_custom_call" | custom-call | flops 16106127360 | bytes 40000000 | tf_op jit(solution)/shard_map/attention_backward/pallas_call | solution.py:897
  312.7 124.0 %last_part.1 = (f32[192,1536]{1,0:T(8,128)}, f32[2,96,1536]{2,1,0:T(8,128)}, bf16[512,1536]{1,0:T(8,128)(2,1)}, f32[8,1536]{1,0:T(8,128)}, f32[48,1536]{1,0:T(8,...) custom-call(bf16[768,1536]{1,0:T(8,128)(2,1)} %get-tuple-element.94.piece_hbm, ...), custom_call_target="tpu_custom_call" | custom-call | flops 10000000000 | bytes 40000000 | tf_op jit(solution)/shard_map/last_part/pallas_call | solution.py:1228
  436.8 0.8 constant_dynamic-slice_fusion
  437.5 0.5 slice_bitcast_fusion
  438.1 1.5 fusion.11
  439.5 3.3 pad_maximum_fusion
  442.9 0.0 collective-permute-done.1
  442.9 0.2 copy-done.2
  443.0 3.3 fusion
  446.3 1.1 copy.39
  447.5 0.7 copy.40
  448.2 0.0 copy-done.4
  448.2 0.7 copy.41
  448.9 1.0 copy.42
  (19 shorter events, 0.1 us)
Async XLA Ops:
  3.6 72.5 %copy-start.6 = (s32[1,1,2,256]{3,1,2,0:T(1,128)}, s32[1,1,2,256]{3,1,2,0:T(1,128)S(1)}, u32[]{:S(2)}) copy-start(s32[1,1,2,256]{3,1,2,0:T(1,128)S(1)} %copy.29) | copy-start | bytes 6148
  171.0 54.3 %collective-permute-start.2 = (bf16[768,1536]{1,0:T(8,128)(2,1)}, bf16[768,1536]{1,0:T(8,128)(2,1)}, u32[]{:S(2)}, u32[]{:S(2)}) collective-permute-start(bf16[768,1536]{1,0:T(8,128)(2,1)} %bitcast.63), channel_id=1, source_target_pairs={{0,16},{16,0},{1,17},{17,1},{2,18},{18,2},{3,19},{19,3},{4,20},{20... | collective-permute-start | bytes 7077896 | tf_op jit(solution)/shard_map/ppermute | solution.py:1251
  172.5 37.2 %collective-permute-start = (bf16[512,1536]{1,0:T(8,128)(2,1)}, bf16[512,1536]{1,0:T(8,128)(2,1)}, u32[]{:S(2)}, u32[]{:S(2)}) collective-permute-start(bf16[512,1536]{1,0:T(8,128)(2,1)} %bitcast.80), channel_id=1, source_target_pairs={{0,2},{1,3},{2,0},{3,1},{4,6},{5,7},{6,4},{7,5},{8,10},{9,11},{10,... | collective-permute-start | bytes 4718600 | tf_op jit(solution)/shard_map/ppermute | solution.py:1256
  209.7 233.1 %collective-permute-start.1 = (bf16[512,1536]{1,0:T(8,128)(2,1)}, bf16[512,1536]{1,0:T(8,128)(2,1)}, u32[]{:S(2)}, u32[]{:S(2)}) collective-permute-start(bf16[512,1536]{1,0:T(8,128)(2,1)} %bitcast.79), channel_id=1, source_target_pairs={{0,2},{1,3},{2,0},{3,1},{4,6},{5,7},{6,4},{7,5},{8,10},{9,11},{10,... | collective-permute-start | bytes 4718600 | tf_op jit(solution)/shard_map/ppermute | solution.py:1256
  439.5 3.3 copy-start
  439.5 3.5 copy-start.2
  443.0 3.3 copy-start.1
  446.3 1.2 copy-start.5
  446.3 1.9 copy-start.4
  446.3 2.6 copy-start.3
